TPU v7x, 512 devices: a whole 4x8x8 slice. The times are simulated.
512 devices in a mesh: row: 32 (over z_hi, x, core), col: 16 (over y, z_lo).
Axes of the slice: x: 4, y: 8, z: 8 (z_hi: 4, z_lo: 2; z = z_hi * 2 + z_lo), core: 2. Of those that a mesh axis runs over, the one named last changes fastest.
Arguments:
- tile_data: bfloat16 [32, 16, 12, 256, 256], P('row', 'col'), may hold values from -1.5 to 1.5
- tile_list: int32 [3, 32, 16, 12], P(None, 'row', 'col'), may hold values from 0 to 4095, as said below
- tile_count: int32 [32, 16], P('row', 'col'), may hold values from 1 to 12, as said below
- current: float32 [8, 1048576], P(None, ('row', 'col'))
- current_image: float32 [8, 1048576], P(None, ('row', 'col'))
- direction: float32 [8, 1048576], P(None, ('row', 'col'))
- direction_image: float32 [8, 1048576], P(None, ('row', 'col'))
- energies: float32 [1048576], P(('row', 'col')), may hold values from 0.2 to 11
- precond: float32 [1048576], P(('row', 'col')), may hold values from 0.2 to 1
- ritz_prev: float32 [8], replicated, may hold values from 0.5 to 3.5
Outputs:
- applied: float32 [8, 1048576], P(None, ('row', 'col'))
- projected: float32 [24, 24], replicated
Inputs may be any that keep to these rules, and one draw needn't show every extreme that they name: `tile_list`: for the device at row index r and col index c, every entry holds a global tile row (component 0) from r * 128 to (r + 1) * 128 - 1, a global tile column (component 1) not above that row whose piece number, column * 256 // 2048, leaves remainder c when divided by 16, and a slot (component 2); the slots of one device are a permutation of 0 to 11. Only a device's first tile_count entries are live. `tile_count`: every device at the last row index has 12 live entries.
All inputs are finite; a program needn't handle non-finite values.
Results may differ from a plain program's by a relative error of at most 0.0003.
Values sent between devices are 32-bit elements; how exact they have to be, the bound alone decides.
A program may use at most 64 MiB of HBM per device.

v0:
```python
import jax
import jax.numpy as jnp
from jax import lax
from jax.sharding import PartitionSpec as P


def apply_tiles(tile_data, tile_list, tile_count, row_res, col_res, piece_len):
    blocks = tile_data[0, 0]
    entries = tile_list[:, 0, 0, :]
    live_count = tile_count[0, 0]
    tile_width = blocks.shape[1]
    per_piece = piece_len // tile_width
    grid_cols = lax.axis_size("col")
    row_first = lax.axis_index("row") * (grid_cols * per_piece)

    def one_tile(entry_at, carry):
        direct, mirror = carry
        slot_index = entries[2, entry_at]
        tile_block = lax.dynamic_index_in_dim(blocks, slot_index, 0, keepdims=False).astype(
            jnp.float32
        )
        is_alive = (entry_at < live_count).astype(jnp.float32)
        local_row = (entries[0, entry_at] - row_first) * tile_width
        col_global = entries[1, entry_at]
        piece_index = col_global // per_piece
        local_col = (piece_index // grid_cols * per_piece + col_global % per_piece) * tile_width
        source_col = lax.dynamic_slice_in_dim(col_res, local_col, tile_width, 1)
        source_row = lax.dynamic_slice_in_dim(row_res, local_row, tile_width, 1)
        direct_term = jnp.dot(source_col, tile_block.T, precision=lax.Precision.HIGHEST) * is_alive
        mirror_term = jnp.dot(source_row, tile_block, precision=lax.Precision.HIGHEST) * is_alive
        direct = lax.dynamic_update_slice_in_dim(
            direct,
            lax.dynamic_slice_in_dim(direct, local_row, tile_width, 1) + direct_term,
            local_row,
            1,
        )
        mirror = lax.dynamic_update_slice_in_dim(
            mirror,
            lax.dynamic_slice_in_dim(mirror, local_col, tile_width, 1) + mirror_term,
            local_col,
            1,
        )
        return (direct, mirror)

    start_direct = jnp.zeros(row_res.shape, jnp.float32)
    start_mirror = jnp.zeros(col_res.shape, jnp.float32)
    return lax.fori_loop(0, blocks.shape[0], one_tile, (start_direct, start_mirror))


def project(gram_h, gram_s):
    symmetric = 0.5 * (gram_h + gram_h.T)
    lower = jnp.linalg.cholesky(gram_s)
    halfway = jax.scipy.linalg.solve_triangular(lower, symmetric, lower=True)
    whitened = jax.scipy.linalg.solve_triangular(lower, halfway.T, lower=True)
    return 0.5 * (whitened + whitened.T)


def body(
    tile_data,
    tile_list,
    tile_count,
    current,
    current_image,
    direction,
    direction_image,
    energies,
    precond,
    ritz_prev,
):
    piece_len = current.shape[1]
    residual = precond[None, :] * (current_image - ritz_prev[:, None] * current)
    row_res = lax.all_gather(residual, "col", axis=1, tiled=True)
    col_res = lax.all_gather(residual, "row", axis=1, tiled=True)
    direct, mirror = apply_tiles(tile_data, tile_list, tile_count, row_res, col_res, piece_len)
    direct_sum = lax.psum_scatter(direct, "col", scatter_dimension=1, tiled=True)
    mirror_sum = lax.psum_scatter(mirror, "row", scatter_dimension=1, tiled=True)
    local_term = energies[None, :] * residual
    applied = local_term + (direct_sum + mirror_sum)
    span_rows = jnp.concatenate([current, residual, direction], 0)
    image_rows = jnp.concatenate([current_image, applied, direction_image], 0)
    gram_h = jnp.dot(span_rows, image_rows.T, precision=lax.Precision.HIGHEST)
    gram_s = jnp.dot(span_rows, span_rows.T, precision=lax.Precision.HIGHEST)
    gram_h, gram_s = lax.psum((gram_h, gram_s), ("row", "col"))
    return (applied, project(gram_h, gram_s))


def solution(mesh):
    in_specs = (
        P("row", "col", None, None, None),
        P(None, "row", "col", None),
        P("row", "col"),
        P(None, ("row", "col")),
        P(None, ("row", "col")),
        P(None, ("row", "col")),
        P(None, ("row", "col")),
        P(("row", "col")),
        P(("row", "col")),
        P(),
    )
    out_specs = (P(None, ("row", "col")), P())
    return jax.shard_map(body, mesh=mesh, in_specs=in_specs, out_specs=out_specs, check_vma=False)
```

profile of v0, /device:TPU:1, one launch (start us, length us, event | category | flops | bytes accessed | tf_op | source)
XLA Modules:
  0.0 540.7 jit_solution(18003749115016480869)
XLA Ops:
  7.2 1.6 subtract_multiply_fusion
  10.3 67.2 %all-gather.5.cloned.1.call-done = f32[8,32768]{1,0:T(8,128)} async-done(((f32[8,2048]{1,0:T(8,128)}), f32[8,32768]{1,0:T(8,128)}) %all-gather.5.cloned.1.call-update) | async-done | bytes 1048592 | tf_op jit(solution)/shard_map/all_gather | solution.py:72
  77.6 75.1 %all-gather.3.cloned.1.call-done = f32[8,65536]{1,0:T(8,128)} async-done(((f32[8,2048]{1,0:T(8,128)}), f32[8,65536]{1,0:T(8,128)}) %all-gather.3.cloned.1.call-update) | async-done | bytes 2097168 | tf_op jit(solution)/shard_map/all_gather | solution.py:73
  152.8 100.8 %while.18 = (s32[]{:T(128)}, f32[8,32768]{1,0:T(8,128)S(1)}, f32[8,65536]{1,0:T(8,128)S(1)}, s32[3,12]{1,0:T(4,128)S(1)}, s32[]{:T(128)}, /*index=5*/f32[8,65536...) while((s32[]{:T(128)}, f32[8,32768]{1,0:T(8,128)S(1)}, ...), condition=%wide.region_1.2_spmd, body=%wide.region_0.1_spmd.sunk | while | flops 12591156 | bytes 312058 | solution.py:47
  159.0 1.1 fusion.43
  160.0 1.1 fusion.42
  167.4 1.1 fusion.43
  168.4 1.1 fusion.42
  175.8 1.1 fusion.43
  176.8 1.1 fusion.42
  184.2 1.1 fusion.43
  185.2 1.1 fusion.42
  192.6 1.1 fusion.43
  193.6 1.1 fusion.42
  201.0 1.1 fusion.43
  202.0 1.1 fusion.42
  209.4 1.1 fusion.43
  210.4 1.1 fusion.42
  217.8 1.1 fusion.43
  218.8 1.1 fusion.42
  226.2 1.1 fusion.43
  227.2 1.1 fusion.42
  234.6 1.1 fusion.43
  235.6 1.1 fusion.42
  243.0 1.1 fusion.43
  244.0 1.1 fusion.42
  252.4 1.1 fusion.42
  255.7 59.2 %reduce-scatter.3.cloned.1.call-done = f32[8,2048]{1,0:T(8,128)} async-done(((f32[8,32768]{1,0:T(8,128)}), f32[8,2048]{1,0:T(8,128)}) %reduce-scatter.3.cloned.1.call-update) | async-done | bytes 65552 | tf_op jit(solution)/shard_map/reduce_scatter | solution.py:75
  314.9 113.2 %reduce-scatter.5.cloned.1.call-done = f32[8,2048]{1,0:T(8,128)} async-done(((f32[8,65536]{1,0:T(8,128)}), f32[8,2048]{1,0:T(8,128)}) %reduce-scatter.5.cloned.1.call-update) | async-done | bytes 65552 | tf_op jit(solution)/shard_map/reduce_scatter | solution.py:76
  429.3 98.2 %all-reduce = (f32[24,24]{0,1:T(8,128)S(1)}, f32[24,24]{0,1:T(8,128)S(1)}) all-reduce(f32[24,24]{0,1:T(8,128)S(1)} %fusion.12, f32[24,24]{0,1:T(8,128)S(1)} %fusion.18), channel_id=1, replica_groups=mesh['row'=32,'col'=16] {'row','col'}, use_global_device_ids=true, to_apply=%region_7.8 | all-reduce | flops 1152 | bytes 9216 | tf_op jit(solution)/shard_map/psum | solution.py:83
  527.6 2.2 cholesky.18
  531.1 1.8 custom-call.8
  (55 shorter events, 17.1 us)
Async XLA Ops:
  7.2 70.4 %all-gather.5.cloned.1.call-start = ((), (), s32[]{:S(2)}) async-start(), calls=%async_computation.3 | async-start | bytes 1114112 | tf_op jit(solution)/shard_map/all_gather | solution.py:72
  8.8 143.8 %all-gather.3.cloned.1.call-start = ((), (), s32[]{:S(2)}) async-start(), calls=%async_computation.2 | async-start | bytes 2162688 | tf_op jit(solution)/shard_map/all_gather | solution.py:73
  9.6 305.3 %reduce-scatter.3.cloned.1.call-start = ((), (), s32[]{:S(2)}) async-start(), calls=%async_computation.4 | async-start | bytes 1114112 | tf_op jit(solution)/shard_map/reduce_scatter | solution.py:75
  253.6 1.1 copy-start.1
  253.7 1.7 copy-start
  253.7 1.7 copy-start.2
  253.7 1.7 copy-start.4
  253.7 1.7 copy-start.8
  253.7 174.4 %copy-start.6 = (f32[2048]{0:T(1024)S(1)}, f32[2048]{0:T(1024)}, u32[]{:S(2)}) copy-start(f32[2048]{0:T(1024)} %param.21) | copy-start | bytes 24580
  253.7 175.3 %copy-start.3 = (f32[8,2048]{1,0:T(8,128)S(1)}, f32[8,2048]{1,0:T(8,128)}, u32[]{:S(2)}) copy-start(f32[8,2048]{1,0:T(8,128)} %param.18) | copy-start | bytes 196612
  253.7 175.3 %copy-start.7 = (f32[8,2048]{1,0:T(8,128)S(1)}, f32[8,2048]{1,0:T(8,128)}, u32[]{:S(2)}) copy-start(f32[8,2048]{1,0:T(8,128)} %param.20) | copy-start | bytes 196612
  254.7 173.4 %reduce-scatter.5.cloned.1.call-start = ((), (), s32[]{:S(2)}) async-start(), calls=%async_computation.5 | async-start | bytes 2162688 | tf_op jit(solution)/shard_map/reduce_scatter | solution.py:76
  429.0 105.2 %copy-start.5 = (f32[8,2048]{1,0:T(8,128)}, f32[8,2048]{1,0:T(8,128)S(1)}, u32[]{:S(2)}) copy-start(f32[8,2048]{1,0:T(8,128)S(1)} %add_add_fusion) | copy-start | bytes 196612
Sparse Core Ops, SparseCore 0:
  10.7 66.8 all-gather.4
  81.3 71.2 all-gather.2
  254.8 60.0 reduce-scatter.2
  319.8 108.2 reduce-scatter.4
where the time goes:
time: 543 us; the launch traced here: 541 us
  waiting for transfers between devices  315 us (58%)
  blocking collectives  98.2 us (18%)
  loops' own time  65.6 us (12%)
  matrix products  27.6 us (5%)
  between operations  14 us (3%)
  local copies, waits for them, and re-layouts  11.2 us (2%)
  other arithmetic  8.45 us (2%)
    reduce_scatter x1, waiting for transfers between devices, body(): lax.psum_scatter(mirror, 'row', scatter_dimension=1, tiled=True)  113 us
    psum x1, blocking collectives, body(): gram_h, gram_s = lax.psum((gram_h, gram_s), ('row', 'col'))  98.2 us
    all_gather x1, waiting for transfers between devices, body(): col_res = lax.all_gather(residual, 'row', axis=1, tiled=True)  75.1 us
    all_gather x1, waiting for transfers between devices, body(): row_res = lax.all_gather(residual, 'col', axis=1, tiled=True)  67.2 us
    another operation x1, loops' own time, apply_tiles(): lax.fori_loop(0, blocks.shape[0], one_tile, (start_direct, start_mirror))  65.6 us
    reduce_scatter x1, waiting for transfers between devices, body(): lax.psum_scatter(direct, 'col', scatter_dimension=1, tiled=True)  59.2 us
    dot_general x12, matrix products, one_tile(): jnp.dot(source_col, tile_block.T, precision=lax.Precision.HIGHEST)  13.8 us
    dot_general x12, matrix products, one_tile(): jnp.dot(source_row, tile_block, precision=lax.Precision.HIGHEST) * is_alive  12.8 us
  transfers between devices with their start and end apart: 4, of which 4 were waited for; matrix products, arithmetic and copies ran while one was open for 0% of the time, Pallas kernels for 0%

commit v1 on v0

v1 whole, which is shorter than its diff:
```python
import jax
import jax.numpy as jnp
from jax import lax
from jax.experimental import pallas as pl
from jax.experimental.pallas import tpu as pltpu
from jax.sharding import PartitionSpec as P

MESH = pl.DeviceIdType.MESH
HIGHEST = lax.Precision.HIGHEST
ZH, XN, YN = 4, 4, 8
NV, B, SUB, T = 8, 256, 8, 12
NT = (((1,), (1,)), ((), ()))
NN = (((1,), (0,)), ((), ()))
TN = (((0,), (0,)), ((), ()))

IDS = {}


def idx(*name):
    return IDS.setdefault(name, len(IDS))


def fill_ids():
    idx("zl")
    for way in (1, -1):
        for s in (1, 2, 3, 4):
            for p in (0, 1):
                idx("y", way, s, p)
                idx("ry", way, s, p)
        for d in range(ZH):
            idx("x", way, d)
            idx("xf", way, d)
            idx("rx2", way, d)
        idx("rx1", way)
    for d in range(1, ZH):
        idx("z", d)
        idx("rz", d)
    for e in range(XN):
        idx("rcore", e)
        for d in range(ZH):
            idx("core", e, d)
    idx("rzl")
    for stage in range(3):
        for d in range(1, 8):
            idx("ar", stage, d)


fill_ids()


def split3(v):
    hi = v.astype(jnp.bfloat16).astype(jnp.float32)
    rest = v - hi
    mid = rest.astype(jnp.bfloat16).astype(jnp.float32)
    low = rest - mid
    return jnp.concatenate([hi, mid, low], 0).astype(jnp.bfloat16)


def split_dot(v, tile, dims):
    out = lax.dot_general(split3(v), tile, dims, preferred_element_type=jnp.float32)
    return (out[16:24] + out[8:16]) + out[0:8]


def kernel(
    tile_hbm, list_s, count_s, cur, cimg, dirn, dimg, en, pre, ritz_s,
    applied, white,
    tiles, rbuf, cbuf, dbuf, mbuf, ry, rcore, rx1, rx2, rz, rzl, pd, pm, gram,
    table_v, table_s, prev_s, send, recv, local_sem,
):
    r = lax.axis_index("row")
    c = lax.axis_index("col")
    zh, x, co = r // 8, (r // 2) % 4, r % 2
    y, zl = c // 2, c % 2

    def dev(zh_, x_, co_, y_, zl_):
        return ((zh_ * 4 + x_) * 2 + co_, y_ * 2 + zl_)

    def at(dz=0, dx=0, dco=0, dy=0, dzl=0):
        return dev((zh + dz) % 4, (x + dx) % 4, (co + dco) % 2, (y + dy) % 8, (zl + dzl) % 2)

    def cx_peer(d):
        q = (x * 2 + co + d) % 8
        return dev(zh, q // 2, q % 2, y, zl)

    def z_peer(d):
        q = (zh * 2 + zl + d) % 8
        return dev(q // 2, x, co, y, q % 2)

    def y_peer(d):
        return dev(zh, x, co, (y + d) % 8, zl)

    tile_copy = pltpu.make_async_copy(tile_hbm.at[0, 0], tiles, local_sem.at[0])
    tile_copy.start()

    barrier = pltpu.get_barrier_semaphore()
    for d in range(1, 8):
        for peer in (cx_peer(d), z_peer(d), y_peer(d)):
            pl.semaphore_signal(barrier, inc=1, device_id=peer, device_id_type=MESH)

    copies = {}

    def go(name, src, dst, target):
        k = idx(*name)
        copy = pltpu.make_async_remote_copy(
            src_ref=src, dst_ref=dst, send_sem=send.at[k], recv_sem=recv.at[k],
            device_id=target, device_id_type=MESH,
        )
        copy.start()
        copies[name] = copy

    def got(*name):
        copies[name].wait_recv()

    rows = lax.broadcasted_iota(jnp.int32, (NV, B), 0)
    ritz = jnp.zeros((NV, B), jnp.float32)
    for a in range(NV):
        ritz = jnp.where(rows == a, ritz_s[a], ritz)
    for s in range(SUB):
        cols = slice(s * B, (s + 1) * B)
        piece = pre[:, cols] * (cimg[:, cols] - ritz * cur[:, cols])
        rbuf[c, s] = piece
        cbuf[co, x, zh, s] = piece

    pl.semaphore_wait(barrier, 21)

    def send_y(s, p, way):
        at_piece = rbuf.at[((y + way * (1 - s)) % 8) * 2 + (zl + p) % 2]
        go(("y", way, s, p), at_piece, at_piece, at(dy=way))

    def send_x(d):
        at_piece = cbuf.at[co, x, (zh - d) % 4]
        for way in (1, -1):
            go(("x", way, d), at_piece, at_piece, at(dx=way))

    def send_core(e, d):
        at_piece = cbuf.at[co, (x - e) % 4, (zh - d) % 4]
        go(("core", e, d), at_piece, at_piece, at(dco=1))

    def forward_x(d):
        way = 1 if d < 2 else -1
        at_piece = cbuf.at[co, (x - way) % 4, (zh - d) % 4]
        go(("xf", way, d), at_piece, at_piece, at(dx=way))

    def arrived_x(d):
        got("x", 1, d)
        got("x", -1, d)
        forward_x(d)
        send_core(1, d)
        send_core(3, d)

    def arrived_z(d):
        got("z", d)
        send_x(d)
        send_core(0, d)

    def arrived_y(s, p, ways=(1, -1)):
        for way in ways:
            got("y", way, s, p)
            send_y(s + 1, p, way)

    own = rbuf.at[c]
    go(("zl",), own, own, at(dzl=1))
    send_y(1, 0, 1)
    send_y(1, 0, -1)
    send_x(0)
    own_c = cbuf.at[co, x, zh]
    for d in (1, 3, 2):
        go(("z", d), own_c, own_c, at(dz=d))
    send_core(0, 0)

    lanes = lax.broadcasted_iota(jnp.int32, (1, 128), 1)
    live = count_s[0, 0]
    row_at = []
    col_at = []
    for k in range(T):
        i = list_s[0, 0, 0, k] & 127
        j = list_s[1, 0, 0, k]
        rr = j >> 7
        row_at.append(i)
        col_at.append((((rr & 1) * 4 + ((rr >> 1) & 3)) * 4 + (rr >> 3)) * 8 + (j & 7))
    tab = [jnp.full((1, 128), T, jnp.int32) for _ in range(3)]
    for k in range(T):
        row_live = jnp.where(k < live, row_at[k], -1)
        col_live = jnp.where(k < live, col_at[k], -1)
        tab[0] = jnp.where(lanes == row_live, k, tab[0])
        tab[1] = jnp.where(lanes == col_live, k, tab[1])
        tab[2] = jnp.where(lanes + 128 == col_live, k, tab[2])
        before_d = jnp.int32(T)
        before_m = jnp.int32(T)
        for q in range(k):
            before_d = jnp.where(row_at[q] == row_at[k], q, before_d)
            before_m = jnp.where(col_at[q] == col_at[k], q, before_m)
        prev_s[0, k] = before_d
        prev_s[1, k] = before_m
    table_v[...] = jnp.zeros_like(table_v)
    for q in range(3):
        table_v[q : q + 1, :] = tab[q]
    table_copy = pltpu.make_async_copy(table_v, table_s, local_sem.at[1])
    table_copy.start()
    pd[T] = jnp.zeros((NV, B), jnp.float32)
    pm[T] = jnp.zeros((NV, B), jnp.float32)

    got("zl")
    send_y(1, 1, 1)
    send_y(1, 1, -1)
    arrived_x(0)
    arrived_y(1, 0)
    arrived_z(1)
    arrived_y(1, 1)
    arrived_z(3)
    arrived_x(1)
    arrived_y(2, 0)
    arrived_z(2)
    arrived_y(2, 1)
    arrived_x(3)
    arrived_y(3, 0, (1,))
    got("y", -1, 3, 0)
    arrived_x(2)
    arrived_y(3, 1, (-1,))
    got("y", 1, 3, 1)
    for d in range(4):
        got("xf", 1 if d < 2 else -1, d)
        send_core(2, d)
    got("y", 1, 4, 0)
    got("y", -1, 4, 1)
    tile_copy.wait()
    table_copy.wait()
    for e in range(XN):
        for d in range(ZH):
            got("core", e, d)

    for k in range(T):
        i = list_s[0, 0, 0, k] & 127
        j = list_s[1, 0, 0, k]
        rr = j >> 7
        tile = tiles[list_s[2, 0, 0, k]]
        source_col = cbuf[rr & 1, (rr >> 1) & 3, rr >> 3, j & 7]
        source_row = rbuf[i >> 3, i & 7]
        pm[k] = split_dot(source_row, tile, NN) + pm[prev_s[1, k]]
        pd[k] = split_dot(source_col, tile, NT) + pd[prev_s[0, k]]

    def fill_m(half, xs):
        def step(q, carry):
            zq = q // 8
            sq = q % 8
            b = ((half * 4 + xs) * 4) * 8 + q
            mbuf[half, xs, zq, sq] = pm[table_s[1 + b // 128, b % 128]]
            return carry

        lax.fori_loop(0, 32, step, 0, unroll=8)

    def fill_d(q, carry):
        dbuf[q // 8, q % 8] = pd[table_s[0, q]]
        return carry

    def add(ref, *others):
        total = ref[...]
        for other in others:
            total = total + other[...]
        ref[...] = total

    for e in (2, 1, 3, 0):
        xs = (x + e) % 4
        fill_m(1 - co, xs)
        go(("rcore", e), mbuf.at[1 - co, xs], rcore.at[xs], at(dco=1))
    lax.fori_loop(0, 128, fill_d, 0, unroll=8)

    def dpiece(dy, p):
        return dbuf.at[((y + dy) % 8) * 2 + (zl + p) % 2]

    def send_ry(s, p, way):
        go(("ry", way, s, p), dpiece(way * (5 - s), p), ry.at[(1 - way) // 2, s - 1, p], at(dy=way))

    def arrived_ry(s, p, way):
        got("ry", way, s, p)
        add(dpiece(way * (4 - s), p), ry.at[(1 - way) // 2, s - 1, p])
        send_ry(s + 1, p, way)

    send_ry(1, 0, 1)
    send_ry(1, 1, -1)
    send_ry(2, 1, 1)
    send_ry(2, 0, -1)
    for e in (2, 1, 3, 0):
        fill_m(co, (x + e) % 4)

    def mpiece(dx, zq):
        return mbuf.at[co, (x + dx) % 4, zq]

    def arrived_core(e):
        got("rcore", e)
        xs = (x + e) % 4
        add(mbuf.at[co, xs], rcore.at[xs])

    arrived_core(2)
    for way in (1, -1):
        half = pl.ds(0 if way == 1 else 2, 2)
        go(("rx1", way), mbuf.at[co, (x + 2) % 4, half], rx1.at[(1 - way) // 2], at(dx=way))

    def send_rx2(zq, way):
        go(("rx2", way, zq), mpiece(way, zq), rx2.at[(1 - way) // 2, zq], at(dx=way))

    arrived_ry(1, 0, 1)
    arrived_ry(1, 1, -1)
    arrived_core(1)
    arrived_core(3)
    send_rx2(2, 1)
    send_rx2(0, -1)
    send_rx2(3, 1)
    send_rx2(1, -1)
    arrived_ry(2, 1, 1)
    arrived_ry(2, 0, -1)
    arrived_core(0)
    got("rx1", 1)
    got("rx1", -1)
    for q in range(2):
        add(mpiece(1, q), rx1.at[0, q])
        send_rx2(q, 1)
        add(mpiece(-1, 2 + q), rx1.at[1, q])
        send_rx2(2 + q, -1)
    arrived_ry(2, 0, 1)
    arrived_ry(2, 1, -1)
    arrived_ry(3, 1, 1)
    arrived_ry(3, 0, -1)

    def arrived_rx2(zq):
        got("rx2", 1, zq)
        got("rx2", -1, zq)
        add(mpiece(0, zq), rx2.at[0, zq], rx2.at[1, zq])

    for zq in range(4):
        arrived_rx2(zq)
    for d in (2, 1, 3):
        go(("rz", d), mbuf.at[co, x, (zh + d) % 4], rz.at[d - 1], at(dz=d))
    arrived_ry(3, 0, 1)
    arrived_ry(3, 1, -1)
    for p in (1, 0):
        got("ry", 1, 4, p)
        got("ry", -1, 4, p)
        add(dpiece(0, p), ry.at[0, 3, p], ry.at[1, 3, p])
        if p == 1:
            go(("rzl",), dpiece(0, 1), rzl, at(dzl=1))
    for d in (1, 3, 2):
        got("rz", d)
    got("rzl")

    for s in range(SUB):
        cols = slice(s * B, (s + 1) * B)
        direct = dbuf[c, s] + rzl[s]
        mirror = (mbuf[co, x, zh, s] + rz[0, s]) + (rz[1, s] + rz[2, s])
        applied[:, cols] = en[:, cols] * rbuf[c, s] + (direct + mirror)

    residual = jnp.concatenate([rbuf[c, s] for s in range(SUB)], 1)
    span = jnp.concatenate([cur[...], residual, dirn[...]], 0)
    images = jnp.concatenate([cimg[...], applied[...], dimg[...]], 0)
    gram[0, 0] = jnp.zeros_like(gram[0, 0])
    gram[0, 0, 0, :, 0:24] = lax.dot_general(span, images, NT, precision=HIGHEST, preferred_element_type=jnp.float32)
    gram[0, 0, 1, :, 0:24] = lax.dot_general(span, span, NT, precision=HIGHEST, preferred_element_type=jnp.float32)
    total = gram[0, 0]
    for stage, peer, me in ((0, cx_peer, x * 2 + co), (1, z_peer, zh * 2 + zl), (2, y_peer, y)):
        gram[1 + stage, me] = total
        for d in range(1, 8):
            mine = gram.at[1 + stage, me]
            go(("ar", stage, d), mine, mine, peer(d))
        for d in range(1, 8):
            got("ar", stage, d)
        total = gram[1 + stage, 0]
        for q in range(1, 8):
            total = total + gram[1 + stage, q]

    gram_h = total[0, :, 0:24]
    gram_s = total[1, :, 0:24]
    at_row = lax.broadcasted_iota(jnp.int32, (24, 24), 0)
    at_col = lax.broadcasted_iota(jnp.int32, (24, 24), 1)
    eye = jnp.where(at_row == at_col, 1.0, 0.0).astype(jnp.float32)
    left, inverse = gram_s, eye
    for k in range(24):
        root = jnp.sqrt(left[k : k + 1, k : k + 1])
        row = left[k : k + 1, :] / root
        row_inverse = inverse[k : k + 1, :] / root
        factor = left[:, k : k + 1] / root
        left = jnp.where(at_row > k, left - factor * row, jnp.where(at_row == k, row, left))
        inverse = jnp.where(
            at_row > k, inverse - factor * row_inverse, jnp.where(at_row == k, row_inverse, inverse)
        )

    def dot(a, b, dims):
        return lax.dot_general(a, b, dims, precision=HIGHEST, preferred_element_type=jnp.float32)

    symmetric = 0.5 * (gram_h + dot(gram_h, eye, TN))
    white[...] = dot(dot(inverse, symmetric, NN), inverse, NT)

    for copy in copies.values():
        copy.wait_send()


def body(
    tile_data, tile_list, tile_count, current, current_image, direction, direction_image,
    energies, precond, ritz_prev,
):
    vmem = pl.BlockSpec(memory_space=pltpu.VMEM)
    smem = pl.BlockSpec(memory_space=pltpu.SMEM)
    f32 = jnp.float32
    n_ids = len(IDS)
    applied, white = pl.pallas_call(
        kernel,
        out_shape=(jax.ShapeDtypeStruct(current.shape, f32), jax.ShapeDtypeStruct((24, 24), f32)),
        in_specs=[pl.BlockSpec(memory_space=pl.ANY), smem, smem, vmem, vmem, vmem, vmem, vmem, vmem, smem],
        out_specs=(vmem, vmem),
        scratch_shapes=[
            pltpu.VMEM((T, B, B), jnp.bfloat16),
            pltpu.VMEM((16, SUB, NV, B), f32),
            pltpu.VMEM((2, XN, ZH, SUB, NV, B), f32),
            pltpu.VMEM((16, SUB, NV, B), f32),
            pltpu.VMEM((2, XN, ZH, SUB, NV, B), f32),
            pltpu.VMEM((2, 4, 2, SUB, NV, B), f32),
            pltpu.VMEM((XN, ZH, SUB, NV, B), f32),
            pltpu.VMEM((2, 2, SUB, NV, B), f32),
            pltpu.VMEM((2, ZH, SUB, NV, B), f32),
            pltpu.VMEM((3, SUB, NV, B), f32),
            pltpu.VMEM((SUB, NV, B), f32),
            pltpu.VMEM((T + 1, NV, B), f32),
            pltpu.VMEM((T + 1, NV, B), f32),
            pltpu.VMEM((4, 8, 2, 24, 128), f32),
            pltpu.VMEM((8, 128), jnp.int32),
            pltpu.SMEM((8, 128), jnp.int32),
            pltpu.SMEM((2, T), jnp.int32),
            pltpu.SemaphoreType.DMA((n_ids,)),
            pltpu.SemaphoreType.DMA((n_ids,)),
            pltpu.SemaphoreType.DMA((2,)),
        ],
        compiler_params=pltpu.CompilerParams(
            collective_id=0, has_side_effects=True, vmem_limit_bytes=40 * 1024 * 1024
        ),
        name="lobpcg_step",
    )(
        tile_data, tile_list, tile_count, current, current_image, direction, direction_image,
        energies.reshape(1, -1), precond.reshape(1, -1), ritz_prev,
    )
    return (applied, 0.5 * (white + white.T))


def solution(mesh):
    in_specs = (
        P("row", "col", None, None, None),
        P(None, "row", "col", None),
        P("row", "col"),
        P(None, ("row", "col")),
        P(None, ("row", "col")),
        P(None, ("row", "col")),
        P(None, ("row", "col")),
        P(("row", "col")),
        P(("row", "col")),
        P(),
    )
    out_specs = (P(None, ("row", "col")), P())
    return jax.shard_map(body, mesh=mesh, in_specs=in_specs, out_specs=out_specs, check_vma=False)
```

time: 543 us -> 94.5 us (0.17)
  waiting for transfers between devices: 315 us -> 0 us
  blocking collectives: 98.2 us -> 0 us
  Pallas kernels: 0 us -> 83 us
  loops' own time: 65.6 us -> 0 us
  matrix products: 27.6 us -> 0 us
  between operations: 14 us -> 1.3 us
  other arithmetic: 8.45 us -> 0.61 us
    reduce_scatter x2 -> x0, waiting for transfers between devices: 172 us -> none  [the longest x1 113 us: body(): lax.psum_scatter(mirror, 'row', scatter_dimension=1, tiled=True)]
    all_gather x2 -> x0, waiting for transfers between devices: 142 us -> none  [the longest x1 75.1 us: body(): col_res = lax.all_gather(residual, 'row', axis=1, tiled=True)]
    psum x1 -> x0, blocking collectives: 98.2 us -> none  [body(): gram_h, gram_s = lax.psum((gram_h, gram_s), ('row', 'col'))]
    pallas_call x0 -> x1, Pallas kernels: none -> 83 us  [body(): pl.pallas_call(kernel, out_shape=(jax.ShapeDtypeStruct(current.shape, f32...]
    another operation x1 -> x0, loops' own time: 65.6 us -> none  [apply_tiles(): lax.fori_loop(0, blocks.shape[0], one_tile, (start_direct, start_mirror))]
    dot_general x26 -> x0, matrix products: 27.1 us -> none  [the longest x12 13.8 us: one_tile(): jnp.dot(source_col, tile_block.T, precision=lax.Precision.HIGHEST)]
    dynamic_slice x12 -> x0, local copies, waits for them, and re-layouts: 8.59 us -> none  [one_tile(): col_global = entries[1, entry_at]]
    unnamed x19, local copies, waits for them, and re-layouts: 2.24 us -> 8.11 us
  transfers between devices with their start and end apart: 4 -> 0, of which waited for: 4 -> 0; matrix products, arithmetic and copies ran while one was open for 0% -> 0% of each run, Pallas kernels for 0% -> 0%
where the time goes in v1:
time: 94.5 us; the launch traced here: 93.1 us
  Pallas kernels  83 us (88%)
  local copies, waits for them, and re-layouts  8.18 us (9%)
  between operations  1.3 us (1%)
    pallas_call x1, Pallas kernels, body(): pl.pallas_call(kernel, out_shape=(jax.ShapeDtypeStruct(current.shape, f32...  83 us
    unnamed x19, local copies, waits for them, and re-layouts  8.11 us

profile of v1, /device:TPU:1, one launch (start us, length us, event | category | flops | bytes accessed | tf_op | source)
XLA Modules:
  0.0 93.1 jit_solution(16097717363453856287)
XLA Ops:
  1.3 0.0 copy-start
  1.3 1.4 %copy-done = bf16[1,1,12,256,256]{4,3,2,1,0:T(8,128)(2,1)S(1)} copy-done((bf16[1,1,12,256,256]{4,3,2,1,0:T(8,128)(2,1)S(1)}, bf16[1,1,12,256,256]{4,3,2,1,0:T(8,128)(2,1)}, u32[]{:S(2)}) %copy-start) | copy-done | bytes 1572888
  2.7 0.0 copy-start.1
  2.7 0.8 copy-done.1
  3.5 0.0 copy-start.2
  3.5 0.8 copy-done.2
  4.4 0.0 copy-start.3
  4.4 0.8 copy-done.3
  5.2 0.0 copy-start.4
  5.2 0.8 copy-done.4
  6.0 0.0 copy-start.5
  6.0 0.7 copy-done.5
  6.7 0.0 copy-start.6
  6.7 0.7 copy-done.6
  7.4 0.0 copy-start.7
  7.4 0.7 copy-done.7
  8.1 0.0 copy-start.8
  8.1 0.7 copy-done.8
  8.8 83.0 %lobpcg_step.1 = (f32[8,2048]{1,0:T(8,128)S(1)}, f32[24,24]{1,0:T(8,128)S(1)}) custom-call(bf16[1,1,12,256,256]{4,3,2,1,0:T(8,128)(2,1)S(1)} %copy-done, s32[3,1,1,12]{3,2,1,0:T(1,128)S(1)} %copy-done.7, s32[1,1]{1,0:T(1,128)S(6)} %copy.14.count_s, f32[8,2048]{1,0:T(8,128)S(1)} %copy-done.1, f32[8,2048]{1,0:T(8,128)S(1)} %copy-done.2, ...), custom_call_target="tpu_custom_call" | custom-call | tf_op jit(solution)/shard_map/lobpcg_step/pallas_call | solution.py:404
  91.7 0.1 copy.12
  91.8 0.6 fusion
  92.4 0.6 copy.15
Async XLA Ops:
  1.3 1.4 %copy-start = (bf16[1,1,12,256,256]{4,3,2,1,0:T(8,128)(2,1)S(1)}, bf16[1,1,12,256,256]{4,3,2,1,0:T(8,128)(2,1)}, u32[]{:S(2)}) copy-start(bf16[1,1,12,256,256]{4,3,2,1,0:T(8,128)(2,1)} %tile_hbm.1) | copy-start | bytes 4718596
  2.7 0.8 copy-start.1
  3.5 0.8 copy-start.2
  4.4 0.8 copy-start.3
  5.2 0.8 copy-start.4
  6.0 0.7 copy-start.5
  6.7 0.7 copy-start.6
  7.4 0.7 copy-start.7
  8.1 0.7 copy-start.8

commit v2 on v1

v2 whole, which is shorter than its diff:
```python
import jax
import jax.numpy as jnp
from jax import lax
from jax.experimental import pallas as pl
from jax.experimental.pallas import tpu as pltpu
from jax.sharding import PartitionSpec as P

MESH = pl.DeviceIdType.MESH
HIGHEST = lax.Precision.HIGHEST
ZH, XN, YN = 4, 4, 8
NV, B, SUB, T = 8, 256, 8, 12
NT = (((1,), (1,)), ((), ()))
NN = (((1,), (0,)), ((), ()))
TN = (((0,), (0,)), ((), ()))

IDS = {}


def idx(*name):
    return IDS.setdefault(name, len(IDS))


def fill_ids():
    idx("zl")
    idx("rzl")
    idx("spl")
    for way in (1, -1):
        for p in (0, 1):
            for step in ("y1", "y2", "y3"):
                idx(step, way, p)
        idx("y4", way)
        for step in ("r1", "r2", "r3", "r4"):
            idx(step, way)
    for d in range(1, ZH):
        idx("z", d)
        idx("rz", d)
        idx("spz", d)
    for e in range(XN):
        idx("rcore", e)
        idx("rx", e)
        for g in range(3):
            idx("x", g, e)
            idx("core", g, e)
    for stage in range(3):
        for d in range(1, 8):
            idx("early", stage, d)
            idx("late", stage, d)


fill_ids()


def split3(v):
    hi = v.astype(jnp.bfloat16).astype(jnp.float32)
    rest = v - hi
    mid = rest.astype(jnp.bfloat16).astype(jnp.float32)
    low = rest - mid
    return jnp.concatenate([hi, mid, low], 0).astype(jnp.bfloat16)


def split_dot(v, tile, dims):
    out = lax.dot_general(split3(v), tile, dims, preferred_element_type=jnp.float32)
    return (out[16:24] + out[8:16]) + out[0:8]


def dot(a, b, dims):
    return lax.dot_general(a, b, dims, precision=HIGHEST, preferred_element_type=jnp.float32)


def cat(ref):
    return jnp.concatenate([ref[s] for s in range(SUB)], 1)


def kernel(
    tile_hbm, list_hbm, count_hbm, cur_hbm, cimg_hbm, dirn_hbm, dimg_hbm, en_hbm, pre_hbm, ritz_hbm,
    applied_hbm, white,
    list_s, count_s, own_cd, cimg, dimg, en, pre, ritz_s, tiles, rbuf, cbuf, dbuf, mbuf,
    ry1, ry2, ry3, ry4, rcore, rx, rz, rzl, spz, spl, pd, pm, early, late, applied,
    table_v, table_s, prev_s, send, recv, local_sem,
):
    r = lax.axis_index("row")
    c = lax.axis_index("col")
    zh, x, co = r // 8, (r // 2) % 4, r % 2
    y, zl = c // 2, c % 2

    def dev(zh_, x_, co_, y_, zl_):
        return ((zh_ * 4 + x_) * 2 + co_, y_ * 2 + zl_)

    def at(dz=0, dx=0, dco=0, dy=0, dzl=0):
        return dev((zh + dz) % 4, (x + dx) % 4, (co + dco) % 2, (y + dy) % 8, (zl + dzl) % 2)

    def cx_peer(d):
        q = (x * 2 + co + d) % 8
        return dev(zh, q // 2, q % 2, y, zl)

    def z_peer(d):
        q = (zh * 2 + zl + d) % 8
        return dev(q // 2, x, co, y, q % 2)

    def y_peer(d):
        return dev(zh, x, co, (y + d) % 8, zl)

    barrier = pltpu.get_barrier_semaphore()
    for d in range(1, 8):
        for peer in (cx_peer(d), z_peer(d), y_peer(d)):
            pl.semaphore_signal(barrier, inc=1, device_id=peer, device_id_type=MESH)

    local = {}
    for q, (name, src, dst) in enumerate((
        ("ritz", ritz_hbm, ritz_s), ("cimg", cimg_hbm, cimg), ("cur", cur_hbm, own_cd.at[0:8]), ("pre", pre_hbm, pre),
        ("list", list_hbm, list_s), ("count", count_hbm, count_s), ("dirn", dirn_hbm, own_cd.at[8:16]),
        ("dimg", dimg_hbm, dimg), ("en", en_hbm, en), ("tiles", tile_hbm.at[0, 0], tiles),
    )):
        local[name] = pltpu.make_async_copy(src, dst, local_sem.at[2 + q])
        local[name].start()

    copies = {}

    def go(name, src, dst, target):
        k = idx(*name)
        copy = pltpu.make_async_remote_copy(
            src_ref=src, dst_ref=dst, send_sem=send.at[k], recv_sem=recv.at[k],
            device_id=target, device_id_type=MESH,
        )
        copy.start()
        copies[name] = copy

    def got(*name):
        copies[name].wait_recv()

    for name in ("ritz", "cimg", "cur", "pre"):
        local.pop(name).wait()
    rows = lax.broadcasted_iota(jnp.int32, (NV, B), 0)
    ritz = jnp.zeros((NV, B), jnp.float32)
    for a in range(NV):
        ritz = jnp.where(rows == a, ritz_s[a], ritz)
    for s in range(SUB):
        cols = slice(s * B, (s + 1) * B)
        piece = pre[:, cols] * (cimg[:, cols] - ritz * own_cd[0:8, cols])
        rbuf[c, s] = piece
        cbuf[co, x, 0, s] = piece

    pl.semaphore_wait(barrier, 21)

    pos = (0, 1, 3, 2)
    group = (pl.ds(0, 1), pl.ds(1, 2), pl.ds(3, 1))

    def rpiece(dy, p):
        return rbuf.at[((y + dy) % 8) * 2 + (zl + p) % 2]

    def send_y(p):
        for step, hops in (("y2", 2), ("y1", 1)):
            for way in (1, -1):
                go((step, way, p), rpiece(0, p), rpiece(0, p), at(dy=hops * way))

    def arrived_y2(p):
        for way in (1, -1):
            got("y2", way, p)
            piece = rpiece(-2 * way, p)
            if p == (1 - way) // 2:
                go(("y4", way), piece, piece, at(dy=2 * way))
            go(("y3", way, p), piece, piece, at(dy=way))

    def send_core(g, e):
        part = cbuf.at[co, (x - e) % 4, group[g]]
        go(("core", g, e), part, part, at(dco=1))

    def send_x(g):
        part = cbuf.at[co, x, group[g]]
        for e in (2, 1, 3):
            go(("x", g, e), part, part, at(dx=e))
        send_core(g, 0)

    def arrived_x(g):
        for e in (1, 3, 2):
            got("x", g, e)
            send_core(g, e)

    own = rpiece(0, 0)
    own_c = cbuf.at[co, x, 0]
    go(("zl",), own, own, at(dzl=1))
    send_y(0)
    for d in (1, 3, 2):
        go(("z", d), own_c, cbuf.at[co, x, pos[d]], at(dz=d))
    send_x(0)

    local.pop("list").wait()
    local.pop("count").wait()
    lanes = lax.broadcasted_iota(jnp.int32, (1, 128), 1)
    live = count_s[0, 0]

    def row_block(k):
        return list_s[0, 0, 0, k] & 127

    def col_block(k):
        j = list_s[1, 0, 0, k]
        owner = j >> 7
        d = (zh - (owner >> 3)) & 3
        return owner & 1, (owner >> 1) & 3, d ^ (d >> 1), j & 7

    row_at = []
    col_at = []
    for k in range(T):
        row_at.append(row_block(k))
        core_k, x_k, pos_k, sub_k = col_block(k)
        col_at.append(((core_k * 4 + x_k) * 4 + pos_k) * 8 + sub_k)
    tab = [jnp.full((1, 128), T, jnp.int32) for _ in range(3)]
    for k in range(T):
        row_live = jnp.where(k < live, row_at[k], -1)
        col_live = jnp.where(k < live, col_at[k], -1)
        tab[0] = jnp.where(lanes == row_live, k, tab[0])
        tab[1] = jnp.where(lanes == col_live, k, tab[1])
        tab[2] = jnp.where(lanes + 128 == col_live, k, tab[2])
        before_d = jnp.int32(T)
        before_m = jnp.int32(T)
        for q in range(k):
            before_d = jnp.where(row_at[q] == row_at[k], q, before_d)
            before_m = jnp.where(col_at[q] == col_at[k], q, before_m)
        prev_s[0, k] = before_d
        prev_s[1, k] = before_m
    table_v[...] = jnp.zeros_like(table_v)
    for q in range(3):
        table_v[q : q + 1, :] = tab[q]
    local["table"] = pltpu.make_async_copy(table_v, table_s, local_sem.at[1])
    local["table"].start()
    pd[T] = jnp.zeros((NV, B), jnp.float32)
    pm[T] = jnp.zeros((NV, B), jnp.float32)

    got("zl")
    send_y(1)

    stages = ((cx_peer, x * 2 + co), (z_peer, zh * 2 + zl), (y_peer, y))

    def share(name, buf, stage, value):
        peer, me = stages[stage]
        buf[stage, me] = value
        for d in (4, 3, 5, 2, 6, 1, 7):
            go((name, stage, d), buf.at[stage, me], buf.at[stage, me], peer(d))

    def shared(name, buf, stage):
        for d in (4, 3, 5, 2, 6, 1, 7):
            got(name, stage, d)
        total = buf[stage, 0]
        for q in range(1, 8):
            total = total + buf[stage, q]
        return total

    for name in ("dirn", "dimg"):
        local.pop(name).wait()
    residual = cat(rbuf.at[c])
    span = jnp.concatenate([own_cd[0:8, :], residual, own_cd[8:16, :]], 0)
    known = jnp.concatenate([cimg[...], jnp.zeros_like(residual), dimg[...], span], 0)
    first = jnp.concatenate([dot(span, known, NT), jnp.zeros((24, 80), jnp.float32)], 1)
    share("early", early, 0, first)

    arrived_x(0)
    arrived_y2(0)
    got("z", 1)
    got("z", 3)
    send_x(1)
    got("z", 2)
    send_x(2)
    arrived_y2(1)
    for d in (2, 1, 3):
        go(("spz", d), own_cd, spz.at[d - 1], at(dz=d))
    go(("spl",), own_cd, spl, at(dzl=1))
    arrived_x(1)
    share("early", early, 1, shared("early", early, 0))
    for way in (1, -1):
        for p in (0, 1):
            got("y1", way, p)
            got("y3", way, p)
        got("y4", way)
    arrived_x(2)
    local.pop("tiles").wait()
    local.pop("table").wait()
    for g in range(3):
        for e in range(XN):
            got("core", g, e)

    for k in range(T):
        i = row_block(k)
        tile = tiles[list_s[2, 0, 0, k]]
        source_col = cbuf[col_block(k)]
        source_row = rbuf[i >> 3, i & 7]
        pd[k] = split_dot(source_col, tile, NT) + pd[prev_s[0, k]]
        pm[k] = split_dot(source_row, tile, NN) + pm[prev_s[1, k]]

    def fill_m(half, xs):
        def step(q, carry):
            b = ((half * 4 + xs) * 4) * 8 + q
            mbuf[half, xs, q // 8, q % 8] = pm[table_s[1 + b // 128, b % 128]]
            return carry

        lax.fori_loop(0, 32, step, 0, unroll=8)

    def fill_d(q, carry):
        dbuf[q // 8, q % 8] = pd[table_s[0, q]]
        return carry

    def add(ref, *others):
        total = ref[...]
        for other in others:
            total = total + other[...]
        ref[...] = total

    def dpair(dy):
        return dbuf.at[pl.ds(((y + dy) % 8) * 2, 2)]

    lax.fori_loop(0, 128, fill_d, 0, unroll=8)
    for way in (1, -1):
        w = (1 - way) // 2
        go(("r3", way), dpair(3 * way), ry3.at[w], at(dy=way))
        go(("r4", way), dbuf.at[((y + 4) % 8) * 2 + (zl + w) % 2], ry4.at[w], at(dy=2 * way))
    for e in (2, 1, 3, 0):
        xs = (x + e) % 4
        fill_m(1 - co, xs)
        go(("rcore", e), mbuf.at[1 - co, xs], rcore.at[xs], at(dco=1))
    for way in (1, -1):
        go(("r1", way), dpair(way), ry1.at[(1 - way) // 2], at(dy=way))
    for e in (2, 1, 3, 0):
        xs = (x + e) % 4
        fill_m(co, xs)
        got("rcore", e)
        add(mbuf.at[co, xs], rcore.at[xs])
        if e:
            go(("rx", e), mbuf.at[co, xs], rx.at[e - 1], at(dx=e))
    share("early", early, 2, shared("early", early, 1))

    for way in (1, -1):
        w = (1 - way) // 2
        got("r3", way)
        got("r4", way)
        add(dpair(2 * way), ry3.at[w])
        add(dbuf.at[((y + 2 * way) % 8) * 2 + (zl + w) % 2], ry4.at[w])
        go(("r2", way), dpair(2 * way), ry2.at[w], at(dy=2 * way))

    total = shared("early", early, 2)
    at_row = lax.broadcasted_iota(jnp.int32, (24, 24), 0)
    at_col = lax.broadcasted_iota(jnp.int32, (24, 24), 1)
    eye = jnp.where(at_row == at_col, 1.0, 0.0).astype(jnp.float32)
    left, inverse = total[:, 24:48], eye
    for k in range(24):
        root = jnp.sqrt(left[k : k + 1, k : k + 1])
        row = left[k : k + 1, :] / root
        row_inverse = inverse[k : k + 1, :] / root
        factor = left[:, k : k + 1] / root
        left = jnp.where(at_row > k, left - factor * row, jnp.where(at_row == k, row, left))
        inverse = jnp.where(
            at_row > k, inverse - factor * row_inverse, jnp.where(at_row == k, row_inverse, inverse)
        )
    white_known = dot(dot(inverse, total[:, 0:24], NN), inverse, NT)

    for d in (1, 2, 3):
        got("spz", d)
    got("spl")
    for e in (1, 2, 3):
        got("rx", e)
    add(mbuf.at[co, x], rx.at[0], rx.at[1], rx.at[2])
    for d in (2, 1, 3):
        go(("rz", d), mbuf.at[co, x, pos[d]], rz.at[d - 1], at(dz=-d))
    for step in ("r1", "r2"):
        for way in (1, -1):
            got(step, way)
    add(dpair(0), ry1.at[0], ry1.at[1], ry2.at[0], ry2.at[1])
    other_c = y * 2 + (1 - zl)
    go(("rzl",), dbuf.at[other_c], rzl, at(dzl=1))

    local.pop("en").wait()
    for s in range(SUB):
        cols = slice(s * B, (s + 1) * B)
        applied[:, cols] = en[:, cols] * rbuf[c, s] + (dbuf[c, s] + mbuf[co, x, 0, s])

    def partial_gram(image, own_span, res):
        return dot(image, jnp.concatenate([own_span[0:8, :], res, own_span[8:16, :]], 0), NT)

    gram = partial_gram(applied[...], own_cd, cat(rbuf.at[c]))
    gram = gram + partial_gram(cat(dbuf.at[other_c]), spl, cat(rbuf.at[other_c]))
    for d in (1, 2, 3):
        gram = gram + partial_gram(cat(mbuf.at[co, x, pos[d]]), spz.at[d - 1], cat(cbuf.at[co, x, pos[d]]))
    gram = jnp.concatenate([gram, jnp.zeros((NV, 104), jnp.float32)], 1)

    share("late", late, 0, gram)
    share("late", late, 2, shared("late", late, 0))
    gram = shared("late", late, 2)
    share("late", late, 1, gram)

    for d in (1, 3, 2):
        got("rz", d)
    got("rzl")
    for s in range(SUB):
        cols = slice(s * B, (s + 1) * B)
        applied[:, cols] = applied[:, cols] + (rzl[s] + (rz[0, s] + rz[1, s] + rz[2, s]))
    local["applied"] = pltpu.make_async_copy(applied, applied_hbm, local_sem.at[0])
    local["applied"].start()
    gram = shared("late", late, 1)[:, 0:24]

    white_all = white_known + dot(inverse[:, 8:16], dot(gram, inverse, NT), NN)
    whitened = 0.5 * (white_all + dot(white_all, eye, TN))
    white[...] = 0.5 * (whitened + dot(whitened, eye, TN))
    local.pop("applied").wait()

    for copy in copies.values():
        copy.wait_send()


def body(
    tile_data, tile_list, tile_count, current, current_image, direction, direction_image,
    energies, precond, ritz_prev,
):
    vmem = pl.BlockSpec(memory_space=pltpu.VMEM)
    hbm = pl.BlockSpec(memory_space=pltpu.HBM)
    f32 = jnp.float32
    n_ids = len(IDS)
    applied, white = pl.pallas_call(
        kernel,
        out_shape=(jax.ShapeDtypeStruct(current.shape, f32), jax.ShapeDtypeStruct((24, 24), f32)),
        in_specs=[hbm] * 10,
        out_specs=(hbm, vmem),
        scratch_shapes=[
            pltpu.SMEM(tile_list.shape, jnp.int32),
            pltpu.SMEM((1, 1), jnp.int32),
            pltpu.VMEM((2 * NV, SUB * B), f32),
            pltpu.VMEM(current.shape, f32),
            pltpu.VMEM(current.shape, f32),
            pltpu.VMEM((1, SUB * B), f32),
            pltpu.VMEM((1, SUB * B), f32),
            pltpu.SMEM((NV,), f32),
            pltpu.VMEM((T, B, B), jnp.bfloat16),
            pltpu.VMEM((16, SUB, NV, B), f32),
            pltpu.VMEM((2, XN, ZH, SUB, NV, B), f32),
            pltpu.VMEM((16, SUB, NV, B), f32),
            pltpu.VMEM((2, XN, ZH, SUB, NV, B), f32),
            pltpu.VMEM((2, 2, SUB, NV, B), f32),
            pltpu.VMEM((2, 2, SUB, NV, B), f32),
            pltpu.VMEM((2, 2, SUB, NV, B), f32),
            pltpu.VMEM((2, SUB, NV, B), f32),
            pltpu.VMEM((XN, ZH, SUB, NV, B), f32),
            pltpu.VMEM((3, ZH, SUB, NV, B), f32),
            pltpu.VMEM((3, SUB, NV, B), f32),
            pltpu.VMEM((SUB, NV, B), f32),
            pltpu.VMEM((3, 2 * NV, SUB * B), f32),
            pltpu.VMEM((2 * NV, SUB * B), f32),
            pltpu.VMEM((T + 1, NV, B), f32),
            pltpu.VMEM((T + 1, NV, B), f32),
            pltpu.VMEM((3, 8, 24, 128), f32),
            pltpu.VMEM((3, 8, NV, 128), f32),
            pltpu.VMEM(current.shape, f32),
            pltpu.VMEM((8, 128), jnp.int32),
            pltpu.SMEM((8, 128), jnp.int32),
            pltpu.SMEM((2, T), jnp.int32),
            pltpu.SemaphoreType.DMA((n_ids,)),
            pltpu.SemaphoreType.DMA((n_ids,)),
            pltpu.SemaphoreType.DMA((12,)),
        ],
        compiler_params=pltpu.CompilerParams(
            collective_id=0, has_side_effects=True, vmem_limit_bytes=60 * 1024 * 1024
        ),
        name="lobpcg_step",
    )(
        tile_data, tile_list, tile_count, current, current_image, direction, direction_image,
        energies.reshape(1, -1), precond.reshape(1, -1), ritz_prev,
    )
    return (applied, white)


def solution(mesh):
    in_specs = (
        P("row", "col", None, None, None),
        P(None, "row", "col", None),
        P("row", "col"),
        P(None, ("row", "col")),
        P(None, ("row", "col")),
        P(None, ("row", "col")),
        P(None, ("row", "col")),
        P(("row", "col")),
        P(("row", "col")),
        P(),
    )
    out_specs = (P(None, ("row", "col")), P())
    return jax.shard_map(body, mesh=mesh, in_specs=in_specs, out_specs=out_specs, check_vma=False)
```

time: 94.5 us -> 75.4 us (0.80); the launches traced: 93.1 us -> 74.9 us
  Pallas kernels: 83 us -> 70.9 us
  local copies, waits for them, and re-layouts: 8.18 us -> 2.78 us
    pallas_call x1, Pallas kernels: 83 us -> 70.9 us  [body(): pl.pallas_call(kernel, out_shape=(jax.ShapeDtypeStruct(current.shape, f32...]
    unnamed x19 -> x2, local copies, waits for them, and re-layouts: 8.11 us -> 2.78 us
where the time goes in v2:
time: 75.4 us; the launch traced here: 74.9 us
  Pallas kernels  70.9 us (94%)
  local copies, waits for them, and re-layouts  2.78 us (4%)
  between operations  1.29 us (2%)
    pallas_call x1, Pallas kernels, body(): pl.pallas_call(kernel, out_shape=(jax.ShapeDtypeStruct(current.shape, f32...  70.9 us
    unnamed x2, local copies, waits for them, and re-layouts  2.78 us

profile of v2, /device:TPU:1, one launch (start us, length us, event | category | flops | bytes accessed | tf_op | source)
XLA Modules:
  0.0 74.9 jit_solution(15773050749234056920)
XLA Ops:
  1.3 70.9 %lobpcg_step.1 = (f32[8,2048]{1,0:T(8,128)}, f32[24,24]{1,0:T(8,128)}) custom-call(bf16[1,1,12,256,256]{4,3,2,1,0:T(8,128)(2,1)} %tile_hbm.1, s32[3,1,1,12]{3,2,1,0:T(1,128)} %list_hbm.1, s32[1,1]{1,0:T(1,128)S(6)} %copy.14.count_hbm, f32[8,2048]{1,0:T(8,128)} %cur_hbm.1, f32[8,2048]{1,0:T(8,128)} %cimg_hbm.1, f32[8,2048]{1,0:T(8,128)} %dirn_hbm.1, ...), custom_call_target="tpu_custom_call" | custom-call | tf_op jit(solution)/shard_map/lobpcg_step/pallas_call | solution.py:415
  72.2 1.5 %copy.15 = f32[8,2048]{1,0:T(8,128)} copy(f32[8,2048]{1,0:T(8,128)} %get-tuple-element.4) | data formatting | bytes 131072
  73.6 1.3 %copy.16 = f32[24,24]{1,0:T(8,128)} copy(f32[24,24]{1,0:T(8,128)} %get-tuple-element.5) | data formatting | bytes 4608

commit v3 on v2

--- a/solution.py
+++ b/solution.py
@@ -31,6 +31,11 @@
         idx("y4", way)
         for step in ("r1", "r2", "r3", "r4"):
             idx(step, way)
+    for d in (1, 3):
+        idx("zf", d)
+        idx("zx", d)
+    idx("rx2", 0)
+    idx("rx2", 3)
     for d in range(1, ZH):
         idx("z", d)
         idx("rz", d)
@@ -38,7 +43,7 @@
     for e in range(XN):
         idx("rcore", e)
         idx("rx", e)
-        for g in range(3):
+        for g in range(4):
             idx("x", g, e)
             idx("core", g, e)
     for stage in range(3):
@@ -73,9 +78,9 @@
 
 def kernel(
     tile_hbm, list_hbm, count_hbm, cur_hbm, cimg_hbm, dirn_hbm, dimg_hbm, en_hbm, pre_hbm, ritz_hbm,
-    applied_hbm, white,
+    applied, white,
     list_s, count_s, own_cd, cimg, dimg, en, pre, ritz_s, tiles, rbuf, cbuf, dbuf, mbuf,
-    ry1, ry2, ry3, ry4, rcore, rx, rz, rzl, spz, spl, pd, pm, early, late, applied,
+    ry1, ry2, ry3, ry4, rcore, rx, rx2, zx, rz, rzl, spz, spl, pd, pm, early, late,
     table_v, table_s, prev_s, send, recv, local_sem,
 ):
     r = lax.axis_index("row")
@@ -101,9 +106,9 @@
         return dev(zh, x, co, (y + d) % 8, zl)
 
     barrier = pltpu.get_barrier_semaphore()
-    for d in range(1, 8):
-        for peer in (cx_peer(d), z_peer(d), y_peer(d)):
-            pl.semaphore_signal(barrier, inc=1, device_id=peer, device_id_type=MESH)
+    near = [at(dz=1), at(dz=3), at(dy=2), at(dy=6), at(dx=2), at(dzl=1), at(dy=1), at(dy=7), at(dx=1), at(dx=3), at(dco=1)]
+    for peer in near:
+        pl.semaphore_signal(barrier, inc=1, device_id=peer, device_id_type=MESH)
 
     local = {}
     for q, (name, src, dst) in enumerate((
@@ -140,10 +145,11 @@
         rbuf[c, s] = piece
         cbuf[co, x, 0, s] = piece
 
-    pl.semaphore_wait(barrier, 21)
+    pl.semaphore_wait(barrier, len(near))
 
     pos = (0, 1, 3, 2)
-    group = (pl.ds(0, 1), pl.ds(1, 2), pl.ds(3, 1))
+    whole = pl.ds(0, 8)
+    group = ((pl.ds(0, 1), whole), (pl.ds(1, 2), whole), (pl.ds(3, 1), pl.ds(0, 4)), (pl.ds(3, 1), pl.ds(4, 4)))
 
     def rpiece(dy, p):
         return rbuf.at[((y + dy) % 8) * 2 + (zl + p) % 2]
@@ -162,11 +168,11 @@
             go(("y3", way, p), piece, piece, at(dy=way))
 
     def send_core(g, e):
-        part = cbuf.at[co, (x - e) % 4, group[g]]
+        part = cbuf.at[(co, (x - e) % 4) + group[g]]
         go(("core", g, e), part, part, at(dco=1))
 
     def send_x(g):
-        part = cbuf.at[co, x, group[g]]
+        part = cbuf.at[(co, x) + group[g]]
         for e in (2, 1, 3):
             go(("x", g, e), part, part, at(dx=e))
         send_core(g, 0)
@@ -179,10 +185,17 @@
     own = rpiece(0, 0)
     own_c = cbuf.at[co, x, 0]
     go(("zl",), own, own, at(dzl=1))
+    for d in (1, 3):
+        go(("z", d), own_c, cbuf.at[co, x, pos[d]], at(dz=d))
     send_y(0)
-    for d in (1, 3, 2):
-        go(("z", d), own_c, cbuf.at[co, x, pos[d]], at(dz=d))
     send_x(0)
+
+    def arrived_z():
+        for d in (1, 3):
+            got("z", d)
+            half = pl.ds(0 if d == 1 else 4, 4)
+            go(("zf", d), cbuf.at[co, x, pos[d], half], cbuf.at[co, x, 3, half], at(dz=d))
+        send_x(1)
 
     local.pop("list").wait()
     local.pop("count").wait()
@@ -245,46 +258,42 @@
             total = total + buf[stage, q]
         return total
 
+    arrived_z()
+    arrived_x(0)
+    arrived_y2(0)
     for name in ("dirn", "dimg"):
         local.pop(name).wait()
     residual = cat(rbuf.at[c])
     span = jnp.concatenate([own_cd[0:8, :], residual, own_cd[8:16, :]], 0)
     known = jnp.concatenate([cimg[...], jnp.zeros_like(residual), dimg[...], span], 0)
     first = jnp.concatenate([dot(span, known, NT), jnp.zeros((24, 80), jnp.float32)], 1)
+
     share("early", early, 0, first)
-
-    arrived_x(0)
-    arrived_y2(0)
-    got("z", 1)
-    got("z", 3)
-    send_x(1)
-    got("z", 2)
+    got("zf", 1)
     send_x(2)
+    got("zf", 3)
+    send_x(3)
     arrived_y2(1)
     for d in (2, 1, 3):
         go(("spz", d), own_cd, spz.at[d - 1], at(dz=d))
     go(("spl",), own_cd, spl, at(dzl=1))
     arrived_x(1)
-    share("early", early, 1, shared("early", early, 0))
     for way in (1, -1):
         for p in (0, 1):
             got("y1", way, p)
             got("y3", way, p)
         got("y4", way)
+    share("early", early, 2, shared("early", early, 0))
     arrived_x(2)
+    arrived_x(3)
     local.pop("tiles").wait()
     local.pop("table").wait()
-    for g in range(3):
+    for g in range(4):
         for e in range(XN):
             got("core", g, e)
 
     for k in range(T):
-        i = row_block(k)
-        tile = tiles[list_s[2, 0, 0, k]]
-        source_col = cbuf[col_block(k)]
-        source_row = rbuf[i >> 3, i & 7]
-        pd[k] = split_dot(source_col, tile, NT) + pd[prev_s[0, k]]
-        pm[k] = split_dot(source_row, tile, NN) + pm[prev_s[1, k]]
+        pd[k] = split_dot(cbuf[col_block(k)], tiles[list_s[2, 0, 0, k]], NT) + pd[prev_s[0, k]]
 
     def fill_m(half, xs):
         def step(q, carry):
@@ -312,6 +321,9 @@
         w = (1 - way) // 2
         go(("r3", way), dpair(3 * way), ry3.at[w], at(dy=way))
         go(("r4", way), dbuf.at[((y + 4) % 8) * 2 + (zl + w) % 2], ry4.at[w], at(dy=2 * way))
+    for k in range(T):
+        i = row_block(k)
+        pm[k] = split_dot(rbuf[i >> 3, i & 7], tiles[list_s[2, 0, 0, k]], NN) + pm[prev_s[1, k]]
     for e in (2, 1, 3, 0):
         xs = (x + e) % 4
         fill_m(1 - co, xs)
@@ -323,9 +335,19 @@
         fill_m(co, xs)
         got("rcore", e)
         add(mbuf.at[co, xs], rcore.at[xs])
-        if e:
-            go(("rx", e), mbuf.at[co, xs], rx.at[e - 1], at(dx=e))
-    share("early", early, 2, shared("early", early, 1))
+        if e == 2:
+            for d in (1, 3):
+                go(("zx", d), mbuf.at[co, xs, pos[d]], zx.at[d // 2], at(dz=-d))
+            go(("rx2", 3), mbuf.at[co, xs, 3], rx2.at[1], at(dx=2))
+        elif e:
+            go(("rx", e), mbuf.at[co, xs], rx.at[e // 2], at(dx=e))
+    got("spl")
+    share("early", early, 1, shared("early", early, 2))
+    far = mbuf.at[co, (x + 2) % 4, 0]
+    for d in (1, 3):
+        got("zx", d)
+    add(far, zx.at[0], zx.at[1])
+    go(("rx2", 0), far, rx2.at[0], at(dx=2))
 
     for way in (1, -1):
         w = (1 - way) // 2
@@ -335,7 +357,7 @@
         add(dbuf.at[((y + 2 * way) % 8) * 2 + (zl + w) % 2], ry4.at[w])
         go(("r2", way), dpair(2 * way), ry2.at[w], at(dy=2 * way))
 
-    total = shared("early", early, 2)
+    total = shared("early", early, 1)
     at_row = lax.broadcasted_iota(jnp.int32, (24, 24), 0)
     at_col = lax.broadcasted_iota(jnp.int32, (24, 24), 1)
     eye = jnp.where(at_row == at_col, 1.0, 0.0).astype(jnp.float32)
@@ -353,10 +375,13 @@
 
     for d in (1, 2, 3):
         got("spz", d)
-    got("spl")
-    for e in (1, 2, 3):
+    for e in (1, 3):
         got("rx", e)
-    add(mbuf.at[co, x], rx.at[0], rx.at[1], rx.at[2])
+    for q in (0, 3):
+        got("rx2", q)
+    add(mbuf.at[co, x], rx.at[0], rx.at[1])
+    add(mbuf.at[co, x, 0], rx2.at[0])
+    add(mbuf.at[co, x, 3], rx2.at[1])
     for d in (2, 1, 3):
         go(("rz", d), mbuf.at[co, x, pos[d]], rz.at[d - 1], at(dz=-d))
     for step in ("r1", "r2"):
@@ -391,17 +416,23 @@
     for s in range(SUB):
         cols = slice(s * B, (s + 1) * B)
         applied[:, cols] = applied[:, cols] + (rzl[s] + (rz[0, s] + rz[1, s] + rz[2, s]))
-    local["applied"] = pltpu.make_async_copy(applied, applied_hbm, local_sem.at[0])
-    local["applied"].start()
     gram = shared("late", late, 1)[:, 0:24]
 
     white_all = white_known + dot(inverse[:, 8:16], dot(gram, inverse, NT), NN)
     whitened = 0.5 * (white_all + dot(white_all, eye, TN))
     white[...] = 0.5 * (whitened + dot(whitened, eye, TN))
-    local.pop("applied").wait()
 
     for copy in copies.values():
         copy.wait_send()
+
+
+def finish(applied, white, applied_out, white_out, sems):
+    first = pltpu.make_async_copy(applied, applied_out, sems.at[0])
+    second = pltpu.make_async_copy(white, white_out, sems.at[1])
+    first.start()
+    second.start()
+    first.wait()
+    second.wait()
 
 
 def body(
@@ -414,9 +445,9 @@
     n_ids = len(IDS)
     applied, white = pl.pallas_call(
         kernel,
-        out_shape=(jax.ShapeDtypeStruct(current.shape, f32), jax.ShapeDtypeStruct((24, 24), f32)),
+        out_shape=(pltpu.VMEM(current.shape, f32), pltpu.VMEM((24, 24), f32)),
         in_specs=[hbm] * 10,
-        out_specs=(hbm, vmem),
+        out_specs=(vmem, vmem),
         scratch_shapes=[
             pltpu.SMEM(tile_list.shape, jnp.int32),
             pltpu.SMEM((1, 1), jnp.int32),
@@ -436,7 +467,9 @@
             pltpu.VMEM((2, 2, SUB, NV, B), f32),
             pltpu.VMEM((2, SUB, NV, B), f32),
             pltpu.VMEM((XN, ZH, SUB, NV, B), f32),
-            pltpu.VMEM((3, ZH, SUB, NV, B), f32),
+            pltpu.VMEM((2, ZH, SUB, NV, B), f32),
+            pltpu.VMEM((2, SUB, NV, B), f32),
+            pltpu.VMEM((2, SUB, NV, B), f32),
             pltpu.VMEM((3, SUB, NV, B), f32),
             pltpu.VMEM((SUB, NV, B), f32),
             pltpu.VMEM((3, 2 * NV, SUB * B), f32),
@@ -445,7 +478,6 @@
             pltpu.VMEM((T + 1, NV, B), f32),
             pltpu.VMEM((3, 8, 24, 128), f32),
             pltpu.VMEM((3, 8, NV, 128), f32),
-            pltpu.VMEM(current.shape, f32),
             pltpu.VMEM((8, 128), jnp.int32),
             pltpu.SMEM((8, 128), jnp.int32),
             pltpu.SMEM((2, T), jnp.int32),

time: 75.4 us -> 71.4 us (0.947)
  Pallas kernels: 70.9 us -> 68.6 us
  local copies, waits for them, and re-layouts: 2.78 us -> 1.23 us
    pallas_call x1, Pallas kernels: 70.9 us -> 68.6 us  [body(): pl.pallas_call(kernel, out_shape=(pltpu.VMEM(current.shape, f32), pltpu.V...]
    unnamed x2, local copies, waits for them, and re-layouts: 2.78 us -> 1.23 us
where the time goes in v3:
time: 71.4 us; the launch traced here: 71.1 us
  Pallas kernels  68.6 us (96%)
  between operations  1.29 us (2%)
  local copies, waits for them, and re-layouts  1.23 us (2%)
    pallas_call x1, Pallas kernels, body(): pl.pallas_call(kernel, out_shape=(pltpu.VMEM(current.shape, f32), pltpu.V...  68.6 us

profile of v3, /device:TPU:1, one launch (start us, length us, event | category | flops | bytes accessed | tf_op | source)
XLA Modules:
  0.0 71.1 jit_solution(10219883068359446855)
XLA Ops:
  1.3 68.6 %lobpcg_step.1 = (f32[8,2048]{1,0:T(8,128)S(1)}, f32[24,24]{1,0:T(8,128)S(1)}) custom-call(bf16[1,1,12,256,256]{4,3,2,1,0:T(8,128)(2,1)} %tile_hbm.1, s32[3,1,1,12]{3,2,1,0:T(1,128)} %list_hbm.1, s32[1,1]{1,0:T(1,128)S(6)} %copy.16.count_hbm, f32[8,2048]{1,0:T(8,128)} %cur_hbm.1, f32[8,2048]{1,0:T(8,128)} %cimg_hbm.1, f32[8,2048]{1,0:T(8,128)} %dirn_hbm.1, ...), custom_call_target="tpu_custom_call" | custom-call | tf_op jit(solution)/shard_map/lobpcg_step/pallas_call | solution.py:446
  69.9 0.6 copy.14
  70.5 0.6 copy.15

commit v4 on v3

--- a/solution.py
+++ b/solution.py
@@ -26,10 +26,9 @@
     idx("spl")
     for way in (1, -1):
         for p in (0, 1):
-            for step in ("y1", "y2", "y3"):
+            for step in ("y1", "y2", "y3", "r1", "r2", "r3"):
                 idx(step, way, p)
-        idx("y4", way)
-        for step in ("r1", "r2", "r3", "r4"):
+        for step in ("y4", "r4"):
             idx(step, way)
     for d in (1, 3):
         idx("zf", d)
@@ -41,11 +40,12 @@
         idx("rz", d)
         idx("spz", d)
     for e in range(XN):
-        idx("rcore", e)
         idx("rx", e)
         for g in range(4):
             idx("x", g, e)
-            idx("core", g, e)
+    idx("codes")
+    idx("need")
+    idx("raw")
     for stage in range(3):
         for d in range(1, 8):
             idx("early", stage, d)
@@ -80,8 +80,8 @@
     tile_hbm, list_hbm, count_hbm, cur_hbm, cimg_hbm, dirn_hbm, dimg_hbm, en_hbm, pre_hbm, ritz_hbm,
     applied, white,
     list_s, count_s, own_cd, cimg, dimg, en, pre, ritz_s, tiles, rbuf, cbuf, dbuf, mbuf,
-    ry1, ry2, ry3, ry4, rcore, rx, rx2, zx, rz, rzl, spz, spl, pd, pm, early, late,
-    table_v, table_s, prev_s, send, recv, local_sem,
+    ry1, ry2, ry3, ry4, rx, rx2, zx, rz, rzl, spz, spl, pd, raw, pm, pack, given, early, late,
+    table_v, table_s, prev_s, code_v, other_v, other_s, send, recv, local_sem,
 ):
     r = lax.axis_index("row")
     c = lax.axis_index("col")
@@ -105,20 +105,25 @@
     def y_peer(d):
         return dev(zh, x, co, (y + d) % 8, zl)
 
+    local = {}
+
+    def load(*items):
+        for name, src, dst in items:
+            local[name] = pltpu.make_async_copy(src, dst, local_sem.at[2 + len(local)])
+            local[name].start()
+
+    load(
+        ("cimg", cimg_hbm, cimg), ("cur", cur_hbm, own_cd.at[0:8]), ("pre", pre_hbm, pre), ("ritz", ritz_hbm, ritz_s),
+    )
     barrier = pltpu.get_barrier_semaphore()
     near = [at(dz=1), at(dz=3), at(dy=2), at(dy=6), at(dx=2), at(dzl=1), at(dy=1), at(dy=7), at(dx=1), at(dx=3), at(dco=1)]
     for peer in near:
         pl.semaphore_signal(barrier, inc=1, device_id=peer, device_id_type=MESH)
 
-    local = {}
-    for q, (name, src, dst) in enumerate((
-        ("ritz", ritz_hbm, ritz_s), ("cimg", cimg_hbm, cimg), ("cur", cur_hbm, own_cd.at[0:8]), ("pre", pre_hbm, pre),
+    load(
         ("list", list_hbm, list_s), ("count", count_hbm, count_s), ("dirn", dirn_hbm, own_cd.at[8:16]),
         ("dimg", dimg_hbm, dimg), ("en", en_hbm, en), ("tiles", tile_hbm.at[0, 0], tiles),
-    )):
-        local[name] = pltpu.make_async_copy(src, dst, local_sem.at[2 + q])
-        local[name].start()
-
+    )
     copies = {}
 
     def go(name, src, dst, target):
@@ -143,13 +148,12 @@
         cols = slice(s * B, (s + 1) * B)
         piece = pre[:, cols] * (cimg[:, cols] - ritz * own_cd[0:8, cols])
         rbuf[c, s] = piece
-        cbuf[co, x, 0, s] = piece
+        cbuf[x * 32 + s] = piece
 
     pl.semaphore_wait(barrier, len(near))
 
     pos = (0, 1, 3, 2)
-    whole = pl.ds(0, 8)
-    group = ((pl.ds(0, 1), whole), (pl.ds(1, 2), whole), (pl.ds(3, 1), pl.ds(0, 4)), (pl.ds(3, 1), pl.ds(4, 4)))
+    group = ((0, 8), (8, 16), (24, 4), (28, 4))
 
     def rpiece(dy, p):
         return rbuf.at[((y + dy) % 8) * 2 + (zl + p) % 2]
@@ -167,34 +171,31 @@
                 go(("y4", way), piece, piece, at(dy=2 * way))
             go(("y3", way, p), piece, piece, at(dy=way))
 
-    def send_core(g, e):
-        part = cbuf.at[(co, (x - e) % 4) + group[g]]
-        go(("core", g, e), part, part, at(dco=1))
+    def cpart(dx, first, size):
+        return cbuf.at[pl.ds(((x + dx) % 4) * 32 + first, size)]
 
     def send_x(g):
-        part = cbuf.at[(co, x) + group[g]]
+        part = cpart(0, *group[g])
         for e in (2, 1, 3):
             go(("x", g, e), part, part, at(dx=e))
-        send_core(g, 0)
 
     def arrived_x(g):
         for e in (1, 3, 2):
             got("x", g, e)
-            send_core(g, e)
 
     own = rpiece(0, 0)
-    own_c = cbuf.at[co, x, 0]
+    own_c = cpart(0, 0, 8)
     go(("zl",), own, own, at(dzl=1))
     for d in (1, 3):
-        go(("z", d), own_c, cbuf.at[co, x, pos[d]], at(dz=d))
+        go(("z", d), own_c, cpart(0, 8 * pos[d], 8), at(dz=d))
     send_y(0)
     send_x(0)
 
     def arrived_z():
         for d in (1, 3):
             got("z", d)
-            half = pl.ds(0 if d == 1 else 4, 4)
-            go(("zf", d), cbuf.at[co, x, pos[d], half], cbuf.at[co, x, 3, half], at(dz=d))
+            half = 0 if d == 1 else 4
+            go(("zf", d), cpart(0, 8 * pos[d] + half, 4), cpart(0, 24 + half, 4), at(dz=d))
         send_x(1)
 
     local.pop("list").wait()
@@ -205,39 +206,42 @@
     def row_block(k):
         return list_s[0, 0, 0, k] & 127
 
-    def col_block(k):
+    def col_code(k):
         j = list_s[1, 0, 0, k]
         owner = j >> 7
         d = (zh - (owner >> 3)) & 3
-        return owner & 1, (owner >> 1) & 3, d ^ (d >> 1), j & 7
-
-    row_at = []
-    col_at = []
+        return (owner & 1) * 128 + (((owner >> 1) & 3) * 4 + (d ^ (d >> 1))) * 8 + (j & 7)
+
+    codes = [col_code(k) for k in range(T)]
+    code_row = jnp.zeros((8, 128), jnp.int32)
+    lanes8 = lax.broadcasted_iota(jnp.int32, (8, 128), 1)
     for k in range(T):
-        row_at.append(row_block(k))
-        core_k, x_k, pos_k, sub_k = col_block(k)
-        col_at.append(((core_k * 4 + x_k) * 4 + pos_k) * 8 + sub_k)
-    tab = [jnp.full((1, 128), T, jnp.int32) for _ in range(3)]
-    for k in range(T):
-        row_live = jnp.where(k < live, row_at[k], -1)
-        col_live = jnp.where(k < live, col_at[k], -1)
-        tab[0] = jnp.where(lanes == row_live, k, tab[0])
-        tab[1] = jnp.where(lanes == col_live, k, tab[1])
-        tab[2] = jnp.where(lanes + 128 == col_live, k, tab[2])
-        before_d = jnp.int32(T)
-        before_m = jnp.int32(T)
-        for q in range(k):
-            before_d = jnp.where(row_at[q] == row_at[k], q, before_d)
-            before_m = jnp.where(col_at[q] == col_at[k], q, before_m)
-        prev_s[0, k] = before_d
-        prev_s[1, k] = before_m
+        code_row = jnp.where(lanes8 == k, codes[k], code_row)
+    code_v[...] = code_row
+    go(("codes",), code_v, other_v, at(dco=1))
+
+    def last_of(keys):
+        found = []
+        for k in range(len(keys)):
+            before = jnp.int32(len(keys))
+            for q in range(k):
+                before = jnp.where(keys[q] == keys[k], q, before)
+            found.append(before)
+        return found
+
+    def table_of(keys):
+        out = jnp.full((1, 128), len(keys), jnp.int32)
+        for k, key in enumerate(keys):
+            out = jnp.where(lanes == key, k, out)
+        return out
+
+    row_at = [row_block(k) for k in range(T)]
+    for k, before in enumerate(last_of(row_at)):
+        prev_s[0, k] = before
     table_v[...] = jnp.zeros_like(table_v)
-    for q in range(3):
-        table_v[q : q + 1, :] = tab[q]
-    local["table"] = pltpu.make_async_copy(table_v, table_s, local_sem.at[1])
-    local["table"].start()
+    table_v[0:1, :] = table_of(row_at)
     pd[T] = jnp.zeros((NV, B), jnp.float32)
-    pm[T] = jnp.zeros((NV, B), jnp.float32)
+    pm[2 * T] = jnp.zeros((NV, B), jnp.float32)
 
     got("zl")
     send_y(1)
@@ -259,6 +263,9 @@
         return total
 
     arrived_z()
+    got("codes")
+    local["codes"] = pltpu.make_async_copy(other_v, other_s, local_sem.at[0])
+    local["codes"].start()
     arrived_x(0)
     arrived_y2(0)
     for name in ("dirn", "dimg"):
@@ -274,31 +281,37 @@
     got("zf", 3)
     send_x(3)
     arrived_y2(1)
-    for d in (2, 1, 3):
-        go(("spz", d), own_cd, spz.at[d - 1], at(dz=d))
+    go(("spz", 2), own_cd, spz.at[1], at(dz=2))
     go(("spl",), own_cd, spl, at(dzl=1))
     arrived_x(1)
-    for way in (1, -1):
-        for p in (0, 1):
-            got("y1", way, p)
-            got("y3", way, p)
-        got("y4", way)
+    local.pop("codes").wait()
+    other_codes = [other_s[0, k] for k in range(T)]
+    keys = [jnp.where(code >> 7 == co, code & 127, -1 - k) for k, code in enumerate(codes + other_codes)]
+    for k, before in enumerate(last_of(keys)):
+        prev_s[1, k] = before
+    table_v[1:2, :] = table_of(keys)
+    local["table"] = pltpu.make_async_copy(table_v, table_s, local_sem.at[1])
+    local["table"].start()
     share("early", early, 2, shared("early", early, 0))
     arrived_x(2)
     arrived_x(3)
+    for k in range(T):
+        pack[k] = cbuf[other_codes[k] & 127]
+    go(("need",), pack, given, at(dco=1))
+    for d in (1, 3):
+        go(("spz", d), own_cd, spz.at[d - 1], at(dz=d))
     local.pop("tiles").wait()
     local.pop("table").wait()
-    for g in range(4):
-        for e in range(XN):
-            got("core", g, e)
+    got("need")
 
     for k in range(T):
-        pd[k] = split_dot(cbuf[col_block(k)], tiles[list_s[2, 0, 0, k]], NT) + pd[prev_s[0, k]]
-
-    def fill_m(half, xs):
+        source = jnp.where(codes[k] >> 7 == co, cbuf[codes[k] & 127], given[k])
+        product = split_dot(source, tiles[list_s[2, 0, 0, k]], NT)
+        pd[k] = jnp.where(k < live, product, 0.0) + pd[prev_s[0, k]]
+
+    def fill_m(xs):
         def step(q, carry):
-            b = ((half * 4 + xs) * 4) * 8 + q
-            mbuf[half, xs, q // 8, q % 8] = pm[table_s[1 + b // 128, b % 128]]
+            mbuf[xs * 32 + q] = pm[table_s[1, xs * 32 + q]]
             return carry
 
         lax.fori_loop(0, 32, step, 0, unroll=8)
@@ -313,37 +326,58 @@
             total = total + other[...]
         ref[...] = total
 
-    def dpair(dy):
-        return dbuf.at[pl.ds(((y + dy) % 8) * 2, 2)]
-
     lax.fori_loop(0, 128, fill_d, 0, unroll=8)
+
+    def dpiece(dy, p):
+        return dbuf.at[((y + dy) % 8) * 2 + (zl + p) % 2]
+
+    def send_r(step, hops, at_y, way, p, buf):
+        go((step, way, p), dpiece(at_y * way, p), buf.at[(1 - way) // 2, p], at(dy=hops * way))
+
+    for way in (1, -1):
+        send_r("r3", 1, 3, way, (1 + way) // 2, ry3)
     for way in (1, -1):
         w = (1 - way) // 2
-        go(("r3", way), dpair(3 * way), ry3.at[w], at(dy=way))
-        go(("r4", way), dbuf.at[((y + 4) % 8) * 2 + (zl + w) % 2], ry4.at[w], at(dy=2 * way))
+        go(("r4", way), dpiece(4, w), ry4.at[w], at(dy=2 * way))
+        send_r("r3", 1, 3, way, w, ry3)
+
+    for way in (1, -1):
+        for p in (0, 1):
+            got("y1", way, p)
+            got("y3", way, p)
+        got("y4", way)
     for k in range(T):
         i = row_block(k)
-        pm[k] = split_dot(rbuf[i >> 3, i & 7], tiles[list_s[2, 0, 0, k]], NN) + pm[prev_s[1, k]]
+        product = split_dot(rbuf[i >> 3, i & 7], tiles[list_s[2, 0, 0, k]], NN)
+        raw[k] = jnp.where(k < live, product, 0.0)
+    go(("raw",), raw.at[pl.ds(0, T)], raw.at[pl.ds(T, T)], at(dco=1))
+    for way in (1, -1):
+        p = (1 + way) // 2
+        got("r3", way, p)
+        add(dpiece(2 * way, p), ry3.at[(1 - way) // 2, p])
+        send_r("r2", 2, 2, way, p, ry2)
+
+    def mpart(dx, first, size):
+        return mbuf.at[pl.ds(((x + dx) % 4) * 32 + first, size)]
+
+    got("raw")
+    for k in range(2 * T):
+        pm[k] = raw[k] + pm[prev_s[1, k]]
     for e in (2, 1, 3, 0):
-        xs = (x + e) % 4
-        fill_m(1 - co, xs)
-        go(("rcore", e), mbuf.at[1 - co, xs], rcore.at[xs], at(dco=1))
-    for way in (1, -1):
-        go(("r1", way), dpair(way), ry1.at[(1 - way) // 2], at(dy=way))
-    for e in (2, 1, 3, 0):
-        xs = (x + e) % 4
-        fill_m(co, xs)
-        got("rcore", e)
-        add(mbuf.at[co, xs], rcore.at[xs])
+        fill_m((x + e) % 4)
         if e == 2:
             for d in (1, 3):
-                go(("zx", d), mbuf.at[co, xs, pos[d]], zx.at[d // 2], at(dz=-d))
-            go(("rx2", 3), mbuf.at[co, xs, 3], rx2.at[1], at(dx=2))
+                go(("zx", d), mpart(2, 8 * pos[d], 8), zx.at[d // 2], at(dz=-d))
+            go(("rx2", 3), mpart(2, 24, 8), rx2.at[1], at(dx=2))
         elif e:
-            go(("rx", e), mbuf.at[co, xs], rx.at[e // 2], at(dx=e))
+            go(("rx", e), mpart(e, 0, 32), rx.at[e // 2], at(dx=e))
+    for way in (1, -1):
+        w = (1 - way) // 2
+        for p in (0, 1):
+            send_r("r1", 1, 1, way, p, ry1)
     got("spl")
     share("early", early, 1, shared("early", early, 2))
-    far = mbuf.at[co, (x + 2) % 4, 0]
+    far = mpart(2, 0, 8)
     for d in (1, 3):
         got("zx", d)
     add(far, zx.at[0], zx.at[1])
@@ -351,11 +385,10 @@
 
     for way in (1, -1):
         w = (1 - way) // 2
-        got("r3", way)
+        got("r3", way, w)
         got("r4", way)
-        add(dpair(2 * way), ry3.at[w])
-        add(dbuf.at[((y + 2 * way) % 8) * 2 + (zl + w) % 2], ry4.at[w])
-        go(("r2", way), dpair(2 * way), ry2.at[w], at(dy=2 * way))
+        add(dpiece(2 * way, w), ry3.at[w, w], ry4.at[w])
+        send_r("r2", 2, 2, way, w, ry2)
 
     total = shared("early", early, 1)
     at_row = lax.broadcasted_iota(jnp.int32, (24, 24), 0)
@@ -379,22 +412,24 @@
         got("rx", e)
     for q in (0, 3):
         got("rx2", q)
-    add(mbuf.at[co, x], rx.at[0], rx.at[1])
-    add(mbuf.at[co, x, 0], rx2.at[0])
-    add(mbuf.at[co, x, 3], rx2.at[1])
+    add(mpart(0, 0, 32), rx.at[0], rx.at[1])
+    add(mpart(0, 0, 8), rx2.at[0])
+    add(mpart(0, 24, 8), rx2.at[1])
     for d in (2, 1, 3):
-        go(("rz", d), mbuf.at[co, x, pos[d]], rz.at[d - 1], at(dz=-d))
-    for step in ("r1", "r2"):
-        for way in (1, -1):
-            got(step, way)
-    add(dpair(0), ry1.at[0], ry1.at[1], ry2.at[0], ry2.at[1])
+        go(("rz", d), mpart(0, 8 * pos[d], 8), rz.at[d - 1], at(dz=-d))
+    for way in (1, -1):
+        for p in (0, 1):
+            got("r1", way, p)
+            got("r2", way, p)
+    for p in (0, 1):
+        add(dpiece(0, p), ry1.at[0, p], ry1.at[1, p], ry2.at[0, p], ry2.at[1, p])
     other_c = y * 2 + (1 - zl)
     go(("rzl",), dbuf.at[other_c], rzl, at(dzl=1))
 
     local.pop("en").wait()
     for s in range(SUB):
         cols = slice(s * B, (s + 1) * B)
-        applied[:, cols] = en[:, cols] * rbuf[c, s] + (dbuf[c, s] + mbuf[co, x, 0, s])
+        applied[:, cols] = en[:, cols] * rbuf[c, s] + (dbuf[c, s] + mbuf[x * 32 + s])
 
     def partial_gram(image, own_span, res):
         return dot(image, jnp.concatenate([own_span[0:8, :], res, own_span[8:16, :]], 0), NT)
@@ -402,7 +437,7 @@
     gram = partial_gram(applied[...], own_cd, cat(rbuf.at[c]))
     gram = gram + partial_gram(cat(dbuf.at[other_c]), spl, cat(rbuf.at[other_c]))
     for d in (1, 2, 3):
-        gram = gram + partial_gram(cat(mbuf.at[co, x, pos[d]]), spz.at[d - 1], cat(cbuf.at[co, x, pos[d]]))
+        gram = gram + partial_gram(cat(mpart(0, 8 * pos[d], 8)), spz.at[d - 1], cat(cpart(0, 8 * pos[d], 8)))
     gram = jnp.concatenate([gram, jnp.zeros((NV, 104), jnp.float32)], 1)
 
     share("late", late, 0, gram)
@@ -459,15 +494,14 @@
             pltpu.SMEM((NV,), f32),
             pltpu.VMEM((T, B, B), jnp.bfloat16),
             pltpu.VMEM((16, SUB, NV, B), f32),
-            pltpu.VMEM((2, XN, ZH, SUB, NV, B), f32),
+            pltpu.VMEM((XN * ZH * SUB, NV, B), f32),
             pltpu.VMEM((16, SUB, NV, B), f32),
-            pltpu.VMEM((2, XN, ZH, SUB, NV, B), f32),
+            pltpu.VMEM((XN * ZH * SUB, NV, B), f32),
             pltpu.VMEM((2, 2, SUB, NV, B), f32),
             pltpu.VMEM((2, 2, SUB, NV, B), f32),
             pltpu.VMEM((2, 2, SUB, NV, B), f32),
             pltpu.VMEM((2, SUB, NV, B), f32),
-            pltpu.VMEM((XN, ZH, SUB, NV, B), f32),
-            pltpu.VMEM((2, ZH, SUB, NV, B), f32),
+            pltpu.VMEM((2, ZH * SUB, NV, B), f32),
             pltpu.VMEM((2, SUB, NV, B), f32),
             pltpu.VMEM((2, SUB, NV, B), f32),
             pltpu.VMEM((3, SUB, NV, B), f32),
@@ -475,12 +509,18 @@
             pltpu.VMEM((3, 2 * NV, SUB * B), f32),
             pltpu.VMEM((2 * NV, SUB * B), f32),
             pltpu.VMEM((T + 1, NV, B), f32),
-            pltpu.VMEM((T + 1, NV, B), f32),
+            pltpu.VMEM((2 * T, NV, B), f32),
+            pltpu.VMEM((2 * T + 1, NV, B), f32),
+            pltpu.VMEM((T, NV, B), f32),
+            pltpu.VMEM((T, NV, B), f32),
             pltpu.VMEM((3, 8, 24, 128), f32),
             pltpu.VMEM((3, 8, NV, 128), f32),
             pltpu.VMEM((8, 128), jnp.int32),
             pltpu.SMEM((8, 128), jnp.int32),
-            pltpu.SMEM((2, T), jnp.int32),
+            pltpu.SMEM((2, 2 * T), jnp.int32),
+            pltpu.VMEM((8, 128), jnp.int32),
+            pltpu.VMEM((8, 128), jnp.int32),
+            pltpu.SMEM((8, 128), jnp.int32),
             pltpu.SemaphoreType.DMA((n_ids,)),
             pltpu.SemaphoreType.DMA((n_ids,)),
             pltpu.SemaphoreType.DMA((12,)),

time: 71.4 us -> 69.6 us (0.975)
  Pallas kernels: 68.6 us -> 66.5 us
    pallas_call x1, Pallas kernels: 68.6 us -> 66.5 us  [body(): pl.pallas_call(kernel, out_shape=(pltpu.VMEM(current.shape, f32), pltpu.V...]
where the time goes in v4:
time: 69.6 us; the launch traced here: 69.1 us
  Pallas kernels  66.5 us (96%)
  between operations  1.29 us (2%)
  local copies, waits for them, and re-layouts  1.23 us (2%)
    pallas_call x1, Pallas kernels, body(): pl.pallas_call(kernel, out_shape=(pltpu.VMEM(current.shape, f32), pltpu.V...  66.5 us

profile of v4, /device:TPU:1, one launch (start us, length us, event | category | flops | bytes accessed | tf_op | source)
XLA Modules:
  0.0 69.1 jit_solution(14304009890968059234)
XLA Ops:
  1.3 66.5 %lobpcg_step.1 = (f32[8,2048]{1,0:T(8,128)S(1)}, f32[24,24]{1,0:T(8,128)S(1)}) custom-call(bf16[1,1,12,256,256]{4,3,2,1,0:T(8,128)(2,1)} %tile_hbm.1, s32[3,1,1,12]{3,2,1,0:T(1,128)} %list_hbm.1, s32[1,1]{1,0:T(1,128)S(6)} %copy.16.count_hbm, f32[8,2048]{1,0:T(8,128)} %cur_hbm.1, f32[8,2048]{1,0:T(8,128)} %cimg_hbm.1, f32[8,2048]{1,0:T(8,128)} %dirn_hbm.1, ...), custom_call_target="tpu_custom_call" | custom-call | tf_op jit(solution)/shard_map/lobpcg_step/pallas_call | solution.py:481
  67.8 0.6 copy.14
  68.5 0.6 copy.15

commit v5 on v4

--- a/solution.py
+++ b/solution.py
@@ -281,7 +281,8 @@
     got("zf", 3)
     send_x(3)
     arrived_y2(1)
-    go(("spz", 2), own_cd, spz.at[1], at(dz=2))
+    for d in (1, 3):
+        go(("spz", d), own_cd, spz.at[d - 1], at(dz=d))
     go(("spl",), own_cd, spl, at(dzl=1))
     arrived_x(1)
     local.pop("codes").wait()
@@ -298,8 +299,7 @@
     for k in range(T):
         pack[k] = cbuf[other_codes[k] & 127]
     go(("need",), pack, given, at(dco=1))
-    for d in (1, 3):
-        go(("spz", d), own_cd, spz.at[d - 1], at(dz=d))
+    go(("spz", 2), own_cd, spz.at[1], at(dz=2))
     local.pop("tiles").wait()
     local.pop("table").wait()
     got("need")

time: 69.6 us -> 69.4 us (level)
  no operation moved by 1% of the time
where the time goes in v5:
time: 69.4 us; the launch traced here: 69.1 us
  Pallas kernels  66.6 us (96%)
  between operations  1.29 us (2%)
  local copies, waits for them, and re-layouts  1.23 us (2%)
    pallas_call x1, Pallas kernels, body(): pl.pallas_call(kernel, out_shape=(pltpu.VMEM(current.shape, f32), pltpu.V...  66.6 us

profile of v5, /device:TPU:1, one launch (start us, length us, event | category | flops | bytes accessed | tf_op | source)
XLA Modules:
  0.0 69.1 jit_solution(743709906452442817)
XLA Ops:
  1.3 66.6 %lobpcg_step.1 = (f32[8,2048]{1,0:T(8,128)S(1)}, f32[24,24]{1,0:T(8,128)S(1)}) custom-call(bf16[1,1,12,256,256]{4,3,2,1,0:T(8,128)(2,1)} %tile_hbm.1, s32[3,1,1,12]{3,2,1,0:T(1,128)} %list_hbm.1, s32[1,1]{1,0:T(1,128)S(6)} %copy.16.count_hbm, f32[8,2048]{1,0:T(8,128)} %cur_hbm.1, f32[8,2048]{1,0:T(8,128)} %cimg_hbm.1, f32[8,2048]{1,0:T(8,128)} %dirn_hbm.1, ...), custom_call_target="tpu_custom_call" | custom-call | tf_op jit(solution)/shard_map/lobpcg_step/pallas_call | solution.py:481
  67.8 0.6 copy.14
  68.5 0.6 copy.15
